TPU v7x, 1024 devices: a whole 4x4x32 slice. The times are simulated.
1024 devices in a mesh: expert: 64 (over z, core), seq: 16 (over y, x).
Axes of the slice: x: 4, y: 4, z: 32, core: 2. Of those that a mesh axis runs over, the one named last changes fastest.
Arguments:
- tokens: bfloat16 [8192, 4096], P('expert', 'seq'), may hold values from -6 to 6
- out_grad: bfloat16 [8192, 4096], P('expert', 'seq'), may hold values from -6 to 6
- expert_ids: int32 [8192, 8], P('expert'), may hold values from 0 to 63, all different within a row; in each aligned block of 128 rows (0 to 127, 128 to 255, ...) at most 20 rows name the same one
- router_probs: float32 [8192, 8], P('expert'), may hold values from 0.05 to 0.5
- keep_mask: int32 [8192, 8], P('expert'), may hold values 0 or 1
- gate_saved: bfloat16 [64, 1280, 768], P('expert', 'seq'), may hold values from -6 to 6
- up_saved: bfloat16 [64, 1280, 768], P('expert', 'seq'), may hold values from -6 to 6
- w_gate: bfloat16 [64, 4096, 768], P('expert', 'seq'), may hold values from -0.09375 to 0.09375
- w_up: bfloat16 [64, 4096, 768], P('expert', 'seq'), may hold values from -0.09375 to 0.09375
- w_down: bfloat16 [64, 768, 4096], P('expert', None, 'seq'), may hold values from -0.21875 to 0.21875
Outputs:
- input_grad: bfloat16 [8192, 4096], P('expert', 'seq')
- gate_wgrad: bfloat16 [64, 4096, 768], P('expert', 'seq')
- up_wgrad: bfloat16 [64, 4096, 768], P('expert', 'seq')
- down_wgrad: bfloat16 [64, 768, 4096], P('expert', None, 'seq')
Inputs may be any that keep to these rules, and one draw needn't show every extreme that they name: `expert_ids`: each row names 8 different experts; within the 128 rows of one block no expert is named by more than 20 rows, a bound that some block reaches.
All inputs are finite; a program needn't handle non-finite values. No bound on the sum of `keep_mask` on one device may be relied on, other than what follows from the above.
Results may differ from a plain program's by a relative error of at most 0.023.
Values may be sent and summed in bfloat16 or wider, within the bound.
A program may use at most 32 MiB of HBM per device.

v0:
```python
import jax
import jax.numpy as jnp
from jax import lax
from jax.sharding import PartitionSpec as P


def swiglu_backward(hidden_grad, gate_in, up_in):
    gate_f = gate_in.astype(jnp.float32)
    up_f = up_in.astype(jnp.float32)
    sigmoid_g = jax.nn.sigmoid(gate_f)
    silu_g = gate_f * sigmoid_g
    hidden = (silu_g * up_f).astype(jnp.bfloat16)
    gate_grad = (hidden_grad * up_f * sigmoid_g * (1.0 + gate_f * (1.0 - sigmoid_g))).astype(
        jnp.bfloat16
    )
    up_grad = (hidden_grad * silu_g).astype(jnp.bfloat16)
    return (hidden, gate_grad, up_grad)


def right_transposed(left, right):
    return lax.dot_general(
        left, right, (((1,), (1,)), ((), ())), preferred_element_type=jnp.float32
    )


def left_transposed(left, right):
    return lax.dot_general(
        left, right, (((0,), (0,)), ((), ())), preferred_element_type=jnp.float32
    )


def per_device(
    tokens,
    out_grad,
    expert_ids,
    router_probs,
    keep_mask,
    gate_saved,
    up_saved,
    w_gate,
    w_up,
    w_down,
):
    owners = lax.axis_size("expert")
    tok_rows, width_part = tokens.shape
    fanout = expert_ids.shape[1]
    experts = w_gate.shape[0] * owners
    share_rows = gate_saved.shape[1]
    slot_total = share_rows * lax.axis_size("seq")
    capacity = slot_total // owners
    routed = expert_ids.reshape(-1)
    onehot = (routed[:, None] == jnp.arange(experts, dtype=jnp.int32)[None, :]).astype(jnp.int32)
    before = jnp.cumsum(onehot, axis=0) - onehot
    position = jnp.sum(before * onehot, axis=1)
    target = routed * capacity + position
    weights = (router_probs * keep_mask.astype(jnp.float32)).reshape(tok_rows, fanout, 1)
    scaled = (
        (weights * out_grad.astype(jnp.float32)[:, None, :])
        .astype(jnp.bfloat16)
        .reshape(-1, width_part)
    )
    spread = jnp.repeat(tokens, fanout, axis=0)
    send_in = jnp.zeros((experts * capacity, width_part), jnp.bfloat16).at[target].set(spread)
    send_grad = jnp.zeros((experts * capacity, width_part), jnp.bfloat16).at[target].set(scaled)
    send_in = send_in.reshape(experts, capacity, width_part)
    send_grad = send_grad.reshape(experts, capacity, width_part)
    recv_in, recv_grad = (
        lax.all_to_all(send_in, "expert", split_axis=0, concat_axis=0, tiled=True),
        lax.all_to_all(send_grad, "expert", split_axis=0, concat_axis=0, tiled=True),
    )
    recv_in = recv_in.reshape(slot_total, width_part)
    recv_grad = recv_grad.reshape(slot_total, width_part)
    down_w = w_down[0]
    gate_w = w_gate[0]
    up_w = w_up[0]
    picked = recv_grad
    hidden_grad = lax.psum_scatter(
        right_transposed(picked, down_w).astype(jnp.bfloat16),
        "seq",
        scatter_dimension=0,
        tiled=True,
    ).astype(jnp.float32)
    hidden, gate_grad, up_grad = swiglu_backward(hidden_grad, gate_saved[0], up_saved[0])
    hidden, gate_grad, up_grad = (
        lax.all_gather(hidden, "seq", axis=0, tiled=True),
        lax.all_gather(gate_grad, "seq", axis=0, tiled=True),
        lax.all_gather(up_grad, "seq", axis=0, tiled=True),
    )
    down_wgrad = left_transposed(hidden, recv_grad).astype(jnp.bfloat16)
    gate_wgrad = left_transposed(recv_in, gate_grad).astype(jnp.bfloat16)
    up_wgrad = left_transposed(recv_in, up_grad).astype(jnp.bfloat16)
    slot_back = (right_transposed(gate_grad, gate_w) + right_transposed(up_grad, up_w)).astype(
        jnp.bfloat16
    )
    slot_back = slot_back.reshape(owners, capacity, width_part)
    arrived = lax.all_to_all(slot_back, "expert", split_axis=0, concat_axis=0, tiled=True).reshape(
        experts * capacity, width_part
    )
    picked = arrived[target].reshape(tok_rows, fanout, width_part)
    input_grad = jnp.sum(picked.astype(jnp.float32), axis=1).astype(jnp.bfloat16)
    return (input_grad, gate_wgrad[None], up_wgrad[None], down_wgrad[None])


def solution(mesh):
    return jax.shard_map(
        per_device,
        mesh=mesh,
        in_specs=(
            P("expert", "seq"),
            P("expert", "seq"),
            P("expert", None),
            P("expert", None),
            P("expert", None),
            P("expert", "seq", None),
            P("expert", "seq", None),
            P("expert", "seq", None),
            P("expert", "seq", None),
            P("expert", None, "seq"),
        ),
        out_specs=(
            P("expert", "seq"),
            P("expert", "seq", None),
            P("expert", "seq", None),
            P("expert", None, "seq"),
        ),
        check_vma=False,
    )
```

profile of v0, /device:TPU:1, one launch (start us, length us, event | category | flops | bytes accessed | tf_op | source)
XLA Modules:
  0.0 545.2 jit_solution(3990334821995438534)
XLA Ops:
  10.0 0.9 convert_element_type.61
  10.9 18.0 %reduce-window.6 = s32[64,8,128]{2,1,0:T(8,128)S(1)} reduce-window(s32[64,8,128]{2,1,0:T(8,128)S(1)} %fusion.21, s32[]{:T(128)} %constant.7.clone.1), window={size=1x1x128 pad=0_0x0_0x127_0}, to_apply=%region_0.0 | reduce-window | flops 8323072 | bytes 524292 | tf_op jit(solution)/shard_map/reduce-window
  29.6 5.6 %scatter_custom_fusion = bf16[1280,256]{1,0:T(8,128)(2,1)S(1)} fusion(s32[1024]{0:T(1024)S(1)} %bitcast.71, f32[128,256]{1,0:T(8,128)S(1)} %convert_element_type.61, f32[1024]{0:T(1024)S(1)} %mul.66, bf16[]{:T(256)} %constant.5.clone.1), kind=kCustom, calls=%fused_computation.14 | custom fusion | flops 524288 | bytes 790530 | tf_op jit(solution)/shard_map/scatter | solution.py:64
  35.3 116.4 %all_to_all.15 = bf16[64,20,256]{2,1,0:T(8,128)(2,1)S(1)} all-to-all(bf16[64,20,256]{2,1,0:T(8,128)(2,1)S(1)} %reshape.90), channel_id=1, replica_groups=mesh['expert'=64,'seq'=16] {'expert'}, dimensions={0} | all-to-all | bytes 1310720 | tf_op jit(solution)/shard_map/all_to_all | solution.py:69
  151.8 2.0 convolution_convert_fusion
  154.0 91.5 %reduce-scatter.2.cloned.1.call-done = bf16[80,768]{1,0:T(8,128)(2,1)} async-done(((bf16[1280,768]{1,0:T(8,128)(2,1)}), bf16[80,768]{1,0:T(8,128)(2,1)}) %reduce-scatter.2.cloned.1.call-update) | async-done | bytes 122896 | tf_op jit(solution)/shard_map/reduce_scatter | solution.py:77
  245.5 1.8 fusion.26
  247.3 5.1 scatter_custom_fusion.1
  252.4 1.0 reshape.96
  253.4 25.4 %all-to-all-start.2 = ((bf16[64,20,256]{2,1,0:T(8,128)(2,1)}), bf16[64,20,256]{2,1,0:T(8,128)(2,1)S(1)}, u32[]{:S(2)}, u32[]{:S(2)}) async-start(bf16[64,20,256]{2,1,0:T(8,128)(2,1)} %reshape.96), calls=%async_computation.3 | async-start | bytes 1572864 | tf_op jit(solution)/shard_map/all_to_all | solution.py:68
  279.6 52.3 %all-gather.4.cloned.1.call-done = bf16[1280,768]{1,0:T(8,128)(2,1)} async-done(((bf16[80,768]{1,0:T(8,128)(2,1)}), bf16[1280,768]{1,0:T(8,128)(2,1)}) %all-gather.4.cloned.1.call-update) | async-done | bytes 1966096 | tf_op jit(solution)/shard_map/all_gather | solution.py:86
  331.9 2.2 fusion.12
  334.2 83.4 %all-gather.6.cloned.1.call-done = bf16[1280,768]{1,0:T(8,128)(2,1)} async-done(((bf16[80,768]{1,0:T(8,128)(2,1)}), bf16[1280,768]{1,0:T(8,128)(2,1)}) %all-gather.6.cloned.1.call-update) | async-done | bytes 1966096 | tf_op jit(solution)/shard_map/all_gather | solution.py:87
  417.5 2.3 fusion
  419.8 1.0 reshape.92
  420.8 24.7 %all-to-all-start.1 = ((bf16[64,20,256]{2,1,0:T(8,128)(2,1)}), bf16[64,20,256]{2,1,0:T(8,128)(2,1)}, u32[]{:S(2)}, u32[]{:S(2)}) async-start(bf16[64,20,256]{2,1,0:T(8,128)(2,1)} %reshape.92), calls=%async_computation.2 | async-start | bytes 1572864 | tf_op jit(solution)/shard_map/all_to_all | solution.py:96
  446.1 1.4 reshape.97
  447.5 3.0 fusion.2
  450.5 1.5 fusion.1
  452.0 77.4 %all-gather.8.cloned.1.call-done = bf16[1280,768]{1,0:T(8,128)(2,1)} async-done(((bf16[80,768]{1,0:T(8,128)(2,1)}), bf16[1280,768]{1,0:T(8,128)(2,1)}) %all-gather.8.cloned.1.call-update) | async-done | bytes 1966096 | tf_op jit(solution)/shard_map/all_gather | solution.py:85
  529.4 3.1 fusion.3
  532.5 1.2 reshape.93
  533.8 3.9 gather_fusion
  537.7 1.0 bitcast_reduce_fusion
  (49 shorter events, 5.1 us)
Async XLA Ops:
  7.2 144.6 %copy-start = (bf16[1,768,256]{2,1,0:T(8,128)(2,1)S(1)}, bf16[1,768,256]{2,1,0:T(8,128)(2,1)}, u32[]{:S(2)}) copy-start(bf16[1,768,256]{2,1,0:T(8,128)(2,1)} %param.19) | copy-start | bytes 1179652
  7.2 238.3 %reduce-scatter.2.cloned.1.call-start = ((), (), s32[]{:S(2)}) async-start(), calls=%async_computation.4 | async-start | bytes 2088960 | tf_op jit(solution)/shard_map/reduce_scatter | solution.py:77
  151.8 2.1 copy-start.3
  151.8 93.7 %copy-start.6 = (bf16[1,80,768]{2,1,0:T(8,128)(2,1)S(1)}, bf16[1,80,768]{2,1,0:T(8,128)(2,1)}, u32[]{:S(2)}) copy-start(bf16[1,80,768]{2,1,0:T(8,128)(2,1)} %param.16) | copy-start | bytes 368644
  151.8 93.7 %copy-start.7 = (bf16[1,80,768]{2,1,0:T(8,128)(2,1)S(1)}, bf16[1,80,768]{2,1,0:T(8,128)(2,1)}, u32[]{:S(2)}) copy-start(bf16[1,80,768]{2,1,0:T(8,128)(2,1)} %param.15) | copy-start | bytes 368644
  153.9 93.4 %copy-start.8 = (bf16[128,256]{1,0:T(8,128)(2,1)S(1)}, bf16[128,256]{1,0:T(8,128)(2,1)}, u32[]{:S(2)}) copy-start(bf16[128,256]{1,0:T(8,128)(2,1)} %param.10) | copy-start | bytes 196612
  153.9 178.0 %all-gather.4.cloned.1.call-start = ((), (), s32[]{:S(2)}) async-start(), calls=%async_computation.5 | async-start | bytes 2088960 | tf_op jit(solution)/shard_map/all_gather | solution.py:86
  247.3 84.6 %copy-start.4 = (bf16[1,256,768]{2,1,0:T(8,128)(2,1)S(1)}, bf16[1,256,768]{2,1,0:T(8,128)(2,1)}, u32[]{:S(2)}) copy-start(bf16[1,256,768]{2,1,0:T(8,128)(2,1)} %param.17) | copy-start | bytes 1179652
  253.4 167.4 %all-to-all-start.2 = ((bf16[64,20,256]{2,1,0:T(8,128)(2,1)}), bf16[64,20,256]{2,1,0:T(8,128)(2,1)S(1)}, u32[]{:S(2)}, u32[]{:S(2)}) async-start(bf16[64,20,256]{2,1,0:T(8,128)(2,1)} %reshape.96), calls=%async_computation.3 | async-start | bytes 1572864 | tf_op jit(solution)/shard_map/all_to_all | solution.py:68
  278.9 138.6 %copy-start.5 = (bf16[1,256,768]{2,1,0:T(8,128)(2,1)S(1)}, bf16[1,256,768]{2,1,0:T(8,128)(2,1)}, u32[]{:S(2)}) copy-start(bf16[1,256,768]{2,1,0:T(8,128)(2,1)} %param.18) | copy-start | bytes 1179652
  278.9 138.6 %all-gather.6.cloned.1.call-start = ((), (), s32[]{:S(2)}) async-start(), calls=%async_computation.6 | async-start | bytes 2088960 | tf_op jit(solution)/shard_map/all_gather | solution.py:87
  420.8 25.3 %copy-start.2 = (bf16[64,20,256]{2,1,0:T(8,128)(2,1)}, bf16[64,20,256]{2,1,0:T(8,128)(2,1)S(1)}, u32[]{:S(2)}) copy-start(bf16[64,20,256]{2,1,0:T(8,128)(2,1)S(1)} %all-to-all-done.2) | copy-start | bytes 1966084
  420.8 111.7 %all-to-all-start.1 = ((bf16[64,20,256]{2,1,0:T(8,128)(2,1)}), bf16[64,20,256]{2,1,0:T(8,128)(2,1)}, u32[]{:S(2)}, u32[]{:S(2)}) async-start(bf16[64,20,256]{2,1,0:T(8,128)(2,1)} %reshape.92), calls=%async_computation.2 | async-start | bytes 1572864 | tf_op jit(solution)/shard_map/all_to_all | solution.py:96
  445.5 83.9 %all-gather.8.cloned.1.call-start = ((), (), s32[]{:S(2)}) async-start(), calls=%async_computation.7 | async-start | bytes 2088960 | tf_op jit(solution)/shard_map/all_gather | solution.py:85
  446.1 4.4 copy-start.1
Sparse Core Ops, SparseCore 0:
  154.0 91.4 reduce-scatter.1
  251.0 80.8 all-gather.3
  337.4 80.0 all-gather.5
  451.5 77.8 all-gather.7
where the time goes:
time: 546 us; the launch traced here: 545 us
  waiting for transfers between devices  306 us (56%)
  blocking collectives  116 us (21%)
  starting transfers between devices  50.5 us (9%)
  other arithmetic  28.9 us (5%)
  local copies, waits for them, and re-layouts  15.8 us (3%)
  matrix products  14.1 us (3%)
  between operations  14 us (3%)
    all_to_all x1, blocking collectives, per_device(): lax.all_to_all(send_grad, 'expert', split_axis=0, concat_axis=0, tiled=True)  116 us
    reduce_scatter x1, waiting for transfers between devices, per_device(): lax.psum_scatter(right_transposed(picked, down_w).astype(jnp.bfloat16), '...  91.5 us
    all_gather x1, waiting for transfers between devices, per_device(): lax.all_gather(up_grad, 'seq', axis=0, tiled=True)  83.4 us
    all_gather x1, waiting for transfers between devices, per_device(): lax.all_gather(hidden, 'seq', axis=0, tiled=True)  77.4 us
    all_gather x1, waiting for transfers between devices, per_device(): lax.all_gather(gate_grad, 'seq', axis=0, tiled=True)  52.3 us
    all_to_all x1, starting transfers between devices, per_device(): lax.all_to_all(send_in, 'expert', split_axis=0, concat_axis=0, tiled=True)  25.4 us
    all_to_all x1, starting transfers between devices, per_device(): lax.all_to_all(slot_back, 'expert', split_axis=0, concat_axis=0, tiled=True)  24.7 us
    another operation x3, other arithmetic  18.2 us
  transfers between devices with their start and end apart: 6, of which 4 were waited for; matrix products, arithmetic and copies ran while one was open for 4% of the time, Pallas kernels for 0%

commit v1 on v0

v1 whole, which is shorter than its diff:
```python
import functools

import jax
import jax.numpy as jnp
from jax import lax
from jax.experimental import pallas as pl
from jax.experimental.pallas import tpu as pltpu
from jax.sharding import PartitionSpec as P

MESH = pl.DeviceIdType.MESH
F32 = jnp.float32
BF16 = jnp.bfloat16


def dot_nt(a, b):
    return lax.dot_general(a, b, (((1,), (1,)), ((), ())), preferred_element_type=F32)


def dot_tn(a, b):
    return lax.dot_general(a, b, (((0,), (0,)), ((), ())), preferred_element_type=F32)


def dot_nn(a, b):
    return lax.dot_general(a, b, (((1,), (0,)), ((), ())), preferred_element_type=F32)


def layer_kernel(
    nz, side, cap,
    tok_ref, og_ref, ids_ref, prob_ref, keep_ref, gate_ref, up_ref, wg_ref, wu_ref, wd_ref,
    ig_ref, gw_ref, uw_ref, dw_ref,
    og_all, tok_all, gu_all, pbuf, rsbuf, hg_all, gg, ug, hid, gs, xs, sb, sbs, pos_ref, contrib, rbuf,
    og_s, og_r, og_ss, og_sr, tk_s, tk_r, tk_ss, tk_sr, gu_s, gu_r, rs_s, rs_r, ag_s, ag_r, sb_s, sb_r,
    cb_s, cb_r,
):
    ns = side * side
    ec = lax.axis_index("expert")
    s = lax.axis_index("seq")
    z, c = ec >> 1, ec & 1
    sy, sx = s // side, s % side
    half_ring = nz // 2
    reach = half_ring // 2
    far = reach + 1
    limit = (half_ring, half_ring - 1)
    n_chunks = nz // 2
    quarter = reach // 2
    tok_rows = og_ref.shape[0]
    rows = 4 * cap
    hw = gate_ref.shape[1] // 2
    per_group = n_chunks // 2

    def at_z(k):
        return (z + k) & (nz - 1)

    def dev(e, q):
        return {"expert": e, "seq": q}

    def remote(src, dst, ssem, rsem, device):
        return pltpu.make_async_remote_copy(
            src, dst, ssem, rsem, device_id=device, device_id_type=MESH
        )

    bar = pltpu.get_barrier_semaphore()
    hops = sorted({1, nz - 1, far, nz - far})
    for k in hops:
        pl.semaphore_signal(bar, inc=1, device_id=dev(at_z(k) * 2 + c, s), device_id_type=MESH)
    pl.semaphore_signal(bar, inc=1, device_id=dev(ec ^ 1, s), device_id_type=MESH)

    def greet(k, carry):
        pl.semaphore_signal(bar, inc=1, device_id=dev(ec, (s + k) & (ns - 1)), device_id_type=MESH)
        return carry

    lax.fori_loop(1, ns, greet, 0)

    weight = prob_ref[...] * keep_ref[...].astype(F32)
    w_hi = weight.astype(BF16).astype(F32)
    w_mid = (weight - w_hi).astype(BF16).astype(F32)
    w_lo = (weight - w_hi) - w_mid
    top = jnp.concatenate([ids_ref[...].astype(F32), w_mid], axis=1)
    low = jnp.concatenate([w_hi, w_lo], axis=1)
    og_all[ec, pl.ds(0, tok_rows), :] = og_ref[...]
    og_all[ec, pl.ds(tok_rows, 16), :] = jnp.concatenate([top, low], axis=0).astype(BF16)
    tok_all[ec] = tok_ref[...]
    for h in range(2):
        gu_all[s, h, 0] = gate_ref[:, h * hw : (h + 1) * hw]
        gu_all[s, h, 1] = up_ref[:, h * hw : (h + 1) * hw]
    pl.semaphore_wait(bar, len(hops) + 1 + ns - 1)

    def zslot(way, d, core):
        return at_z(nz - d if way == 0 else d) * 2 + core

    def ring_send(buf, ssem, rsem, way, d, child):
        k = child - d
        slot = zslot(way, d, c)
        target = at_z(k if way == 0 else nz - k) * 2 + c
        return remote(
            buf.at[slot], buf.at[slot], ssem.at[way, child], rsem.at[way, child], dev(target, s)
        )

    def ring_landed(buf, ssem, rsem, way, d):
        slot = buf.at[zslot(way, d, c)]
        remote(slot, slot, ssem.at[way, d], rsem.at[way, d], dev(ec, s)).wait_recv()

    def sib_copy(buf, ssem, rsem, way, d, core):
        slot = buf.at[zslot(way, d, core)]
        return remote(slot, slot, ssem.at[way, d], rsem.at[way, d], dev(ec ^ 1, s))

    og_x = (og_all, og_s, og_r)
    og_sib = (og_all, og_ss, og_sr)
    tk_x = (tok_all, tk_s, tk_r)
    tk_sib = (tok_all, tk_ss, tk_sr)

    for way in (0, 1):
        ring_send(*og_x, way, 0, 1).start()
        ring_send(*og_x, way, 0, far).start()
    sib_copy(*og_sib, 0, 0, c).start()

    def seq_of(y, x):
        return (y & (side - 1)) * side + (x & (side - 1))

    def gu_peer(h, phase, k):
        return seq_of(sy, sx + k) if (h == phase) else seq_of(sy + k, sx)

    def gu_slot(h, j):
        return seq_of(sy, sx + j) if h == 0 else seq_of(sy + j, sx)

    def gu_first(h, k):
        return remote(
            gu_all.at[s, h], gu_all.at[s, h], gu_s.at[h, 0, k], gu_r.at[h, 0, k],
            dev(ec, gu_peer(h, 0, k)),
        )

    def gu_second(h, j, k):
        slot = gu_all.at[gu_slot(h, j), h]
        return remote(
            slot, slot, gu_s.at[h, 1 + j, k], gu_r.at[h, 1 + j, k], dev(ec, gu_peer(h, 1, k))
        )

    def gu_landed(slot, h, a, k):
        ref = gu_all.at[slot, h]
        remote(ref, ref, gu_s.at[h, a, k], gu_r.at[h, a, k], dev(ec, s)).wait_recv()

    for k in range(1, side):
        for h in range(2):
            gu_first(h, k).start()
    for k in range(1, side):
        for h in range(2):
            gu_second(h, 0, k).start()
    for way in (0, 1):
        ring_send(*tk_x, way, 0, 1).start()
    sib_copy(*tk_sib, 0, 0, c).start()

    def og_step(k):
        for way in (0, 1):
            ring_landed(*og_x, way, k)

            @pl.when(k < reach)
            def _():
                ring_send(*og_x, way, k, k + 1).start()

            sib_copy(*og_sib, way, k, c).start()

            def far_part():
                ring_landed(*og_x, way, reach + k)

                @pl.when(reach + k < limit[way])
                def _():
                    ring_send(*og_x, way, reach + k, reach + k + 1).start()

                sib_copy(*og_sib, way, reach + k, c).start()

            if way == 0:
                far_part()
            else:
                pl.when(reach + k <= limit[1])(far_part)

    def og_sib_wait(k):
        for way in (0, 1):
            sib_copy(*og_sib, way, k, 1 - c).wait_recv()
            if way == 0:
                sib_copy(*og_sib, way, reach + k, 1 - c).wait_recv()
            else:

                @pl.when(reach + k <= limit[1])
                def _():
                    sib_copy(*og_sib, way, reach + k, 1 - c).wait_recv()

    def tok_step(d, carry):
        for way in (0, 1):

            def part():
                ring_landed(*tk_x, way, d)

                @pl.when(d < limit[way])
                def _():
                    ring_send(*tk_x, way, d, d + 1).start()

                sib_copy(*tk_sib, way, d, c).start()

            if way == 0:
                part()
            else:
                pl.when(d <= limit[1])(part)
        return carry

    row80 = lax.broadcasted_iota(jnp.int32, (rows, tok_rows), 0).astype(F32)
    row8 = lax.broadcasted_iota(jnp.int32, (8, tok_rows), 0)
    before = (
        lax.broadcasted_iota(jnp.int32, (tok_rows, tok_rows), 0)
        < lax.broadcasted_iota(jnp.int32, (tok_rows, tok_rows), 1)
    ).astype(F32).astype(BF16)

    def chunk_at(offset):
        return ((z >> 1) + offset) & (n_chunks - 1)

    def chunk_of(o):
        m = ((o - 1) >> 2) + 1
        r = (o - 1) & 3
        last = o - (n_chunks - 3)
        plain = (m + jnp.where(r >= 2, quarter, 0)) * jnp.where((r & 1) == 1, -1, 1)
        tail = jnp.where(last == 0, quarter, jnp.where(last == 1, -quarter, n_chunks // 2))
        off = jnp.where(o == 0, 0, jnp.where(last >= 0, tail, plain))
        return chunk_at(off + n_chunks)

    def pick(o, carry):
        i = chunk_of(o)
        member = jnp.zeros((8, tok_rows), F32)
        ws = []
        for q in range(4):
            meta = og_all[4 * i + q, pl.ds(tok_rows, 16), :].astype(F32)
            ids = meta[0:8, 0:tok_rows]
            w = (meta[8:16, 0:tok_rows] + meta[0:8, tok_rows:]) + meta[8:16, tok_rows:]
            for t in range(2):
                own = (ids == (ec if t == 0 else ec ^ 1).astype(F32)).astype(F32)
                member = jnp.where(
                    row8 == t * 4 + q, jnp.sum(own, axis=0, keepdims=True), member
                )
                if t == 0:
                    ws.append(jnp.sum(own * w, axis=0, keepdims=True))
        count = dot_nn(member.astype(BF16), before)
        place = jnp.where(member > 0.5, count + ((row8 & 3) * cap).astype(F32), -1000.0)
        pos_ref[i] = place
        total = jnp.zeros((rows, og_ref.shape[1]), F32)
        wsum = jnp.zeros((rows, 1), F32)
        for q in range(4):
            hot = (row80 == place[q : q + 1, :]).astype(F32)
            total += dot_nn(hot.astype(BF16), og_all[4 * i + q, pl.ds(0, tok_rows), :])
            wsum += jnp.sum(hot * ws[q], axis=1, keepdims=True)
        gs[o] = (total * wsum).astype(BF16)
        return carry

    def partial_products(m, count):
        left = gs[pl.ds(m, count)].reshape(count * rows, gs.shape[2])
        out = dot_nt(left, wd_ref[...]).astype(BF16)
        for r in range(count):
            o = m + r
            for h in range(2):
                pbuf[o * 2 + h] = out[r * rows : (r + 1) * rows, h * hw : (h + 1) * hw]

    def rs_copy(g, k):
        j = (s + k) & (ns - 1)
        return remote(
            pbuf.at[g * ns + j], rsbuf.at[g, s], rs_s.at[g, k], rs_r.at[g, k], dev(ec, j)
        )

    def rs_start(g):
        def go(k, carry):
            rs_copy(g, k).start()
            return carry

        lax.fori_loop(1, ns, go, 0)
        rsbuf[g, s] = pbuf[g * ns + s]

    def ag_copy(g, k):
        piece = hg_all.at[g * ns + s]
        return remote(piece, piece, ag_s.at[g, k], ag_r.at[g, k], dev(ec, (s + k) & (ns - 1)))

    def rs_finish(g):
        def landed(k, carry):
            slot = rsbuf.at[g, (s - k) & (ns - 1)]
            remote(slot, slot, rs_s.at[g, k], rs_r.at[g, k], dev(ec, s)).wait_recv()
            return carry

        lax.fori_loop(1, ns, landed, 0)

        def add(r, carry):
            band = pl.ds(pl.multiple_of(r * 16, 16), 16)
            total = rsbuf[g, 0, band, :].astype(F32)
            for j in range(1, ns):
                total += rsbuf[g, j, band, :].astype(F32)
            hg_all[g * ns + s, band, :] = total.astype(BF16)
            return carry

        lax.fori_loop(0, rows // 16, add, 0)

        def go(k, carry):
            ag_copy(g, k).start()
            return carry

        lax.fori_loop(1, ns, go, 0)

    def sb_copy(i):
        return remote(sb.at[i], sbs.at[i], sb_s.at[i], sb_r.at[i], dev(ec ^ 1, s))

    def activations(g):
        def landed(k, carry):
            slot = hg_all.at[g * ns + ((s - k) & (ns - 1))]
            remote(slot, slot, ag_s.at[g, k], ag_r.at[g, k], dev(ec, s)).wait_recv()
            return carry

        lax.fori_loop(1, ns, landed, 0)

        def act(p, carry):
            o = p // (rows // 16)
            band = pl.ds(pl.multiple_of((p % (rows // 16)) * 16, 16), 16)
            i = chunk_of(o)
            for h in range(2):
                lanes = pl.ds(h * hw, hw)
                grad = hg_all[o * 2 + h, band, :].astype(F32)
                gate = gu_all[i, h, 0, band, :].astype(F32)
                up = gu_all[i, h, 1, band, :].astype(F32)
                sig = jax.nn.sigmoid(gate)
                silu = gate * sig
                hid[o, band, lanes] = (silu * up).astype(BF16)
                gg[o, band, lanes] = (grad * up * sig * (1.0 + gate * (1.0 - sig))).astype(BF16)
                ug[o, band, lanes] = (grad * silu).astype(BF16)
            return carry

        n_bands = per_group * (rows // 16)
        lax.fori_loop(g * n_bands, (g + 1) * n_bands, act, 0)
        o0 = g * per_group
        shape = (per_group * rows, gg.shape[2])
        back = dot_nt(gg[pl.ds(o0, per_group)].reshape(shape), wg_ref[...]) + dot_nt(
            ug[pl.ds(o0, per_group)].reshape(shape), wu_ref[...]
        )
        back = back.astype(BF16)
        for r in range(per_group):
            i = chunk_of(o0 + r)
            sb[i] = back[r * rows : (r + 1) * rows]
            sb_copy(i).start()

    og_step(1)
    sib_copy(*og_sib, 0, 0, 1 - c).wait_recv()
    og_sib_wait(1)
    lax.fori_loop(0, 1, pick, 0)
    for k in range(1, side):
        for h in range(2):
            j = side - k
            gu_landed(gu_slot(h, j), h, 0, k)
            for k2 in range(1, side):
                gu_second(h, j, k2).start()
    tok_step(1, 0)

    def two_steps(m, carry):
        og_step(2 * m)
        tok_step(2 * m, 0)
        og_step(2 * m + 1)
        og_sib_wait(2 * m)
        og_sib_wait(2 * m + 1)
        tok_step(2 * m + 1, 0)
        lax.fori_loop(4 * m - 3, 4 * m + 1, pick, 0)
        partial_products(4 * m - 4, 4)
        return carry

    lax.fori_loop(1, quarter - 1, two_steps, 0)
    rs_start(0)
    two_steps(quarter - 1, 0)
    og_step(reach)
    og_sib_wait(reach)
    lax.fori_loop(n_chunks - 3, n_chunks, pick, 0)
    partial_products(n_chunks - 4, 4)
    rs_start(1)
    rs_finish(0)
    tok_step(reach, 0)
    tok_step(reach + 1, 0)
    rs_finish(1)
    lax.fori_loop(reach + 2, reach + 5, tok_step, 0)
    for k in range(1, side):
        for h in range(2):
            for j in range(side):
                m = side - k
                slot = seq_of(sy + m, sx + j) if h == 0 else seq_of(sy + j, sx + m)
                gu_landed(slot, h, 1 + j, k)
    activations(0)
    activations(1)
    lax.fori_loop(reach + 5, half_ring + 1, tok_step, 0)

    def contribution(chip):
        i = chip >> 1
        q = ((chip & 1) << 1) + c
        place = pos_ref[i]
        total = jnp.zeros((tok_rows, ig_ref.shape[1]), F32)
        for t, rowsrc in ((0, sb), (1, sbs)):
            mine = jnp.sum(jnp.where(row8 == t * 4 + q, place, 0.0), axis=0, keepdims=True)
            hot = (row80 == mine).astype(F32).astype(BF16)
            total += dot_tn(hot, rowsrc[i])
        return total

    def sb_landed(i, carry):
        sb_copy(i).wait_recv()
        return carry

    lax.fori_loop(0, n_chunks, sb_landed, 0)

    def target(way, chain, k):
        d = (reach if chain == 0 else half_ring) - k
        return at_z(d if way == 0 else nz - d), d

    def cb_copy(way, chain, k):
        chip, d = target(way, chain, k)
        hop = jnp.where((chain == 1) & (k == reach - 1), far, 1)
        nxt = at_z(jnp.where(way == 0, hop, nz - hop)) * 2 + c
        return remote(
            contrib.at[chip], rbuf.at[way, chain, k + 1], cb_s.at[way, chain, k],
            cb_r.at[way, chain, k + 1], dev(nxt, s),
        )

    def cb_landed(way, chain, k):
        slot = rbuf.at[way, chain, k]
        remote(slot, slot, cb_s.at[way, chain, 0], cb_r.at[way, chain, k], dev(ec, s)).wait_recv()

    chains = ((0, 0), (1, 0), (0, 1), (1, 1))

    def prepare(k):
        for way, chain in chains:
            chip, _ = target(way, chain, k)
            contrib[chip] = contribution(chip).astype(BF16)

    for way, chain in chains:
        if (way, chain) != (1, 1):
            chip, _ = target(way, chain, 0)
            contrib[chip] = contribution(chip).astype(BF16)
            cb_copy(way, chain, 0).start()

    def pick_tokens(o, carry):
        i = chunk_of(o)
        place = pos_ref[i]
        total = jnp.zeros((rows, tok_ref.shape[1]), F32)
        for q in range(4):
            hot = (row80 == place[q : q + 1, :]).astype(F32).astype(BF16)
            total += dot_nn(hot, tok_all[4 * i + q])
        xs[o] = total.astype(BF16)
        return carry

    def flat(ref):
        return ref[...].reshape(n_chunks * rows, ref.shape[2])

    def combine(k, carry):
        prepare(k)
        for way, chain in chains:

            def receive():
                chip, _ = target(way, chain, k)
                cb_landed(way, chain, k)
                contrib[chip] = (
                    contrib[chip].astype(F32) + rbuf[way, chain, k].astype(F32)
                ).astype(BF16)

            if (way, chain) == (1, 1):
                pl.when(k > 1)(receive)
            else:
                receive()
            cb_copy(way, chain, k).start()
        return carry

    combine(1, 0)
    sib_copy(*tk_sib, 0, 0, 1 - c).wait_recv()

    def tok_sib_wait(d, carry):
        sib_copy(*tk_sib, 0, d, 1 - c).wait_recv()

        @pl.when(d <= limit[1])
        def _():
            sib_copy(*tk_sib, 1, d, 1 - c).wait_recv()

        return carry

    lax.fori_loop(1, half_ring + 1, tok_sib_wait, 0)
    lax.fori_loop(0, n_chunks // 2, pick_tokens, 0)
    lax.fori_loop(2, min(3, reach), combine, 0)
    lax.fori_loop(n_chunks // 2, n_chunks, pick_tokens, 0)
    lax.fori_loop(min(3, reach), min(4, reach), combine, 0)
    gw_ref[...] = dot_tn(flat(xs), flat(gg)).astype(BF16)
    lax.fori_loop(min(4, reach), min(5, reach), combine, 0)
    uw_ref[...] = dot_tn(flat(xs), flat(ug)).astype(BF16)
    lax.fori_loop(min(5, reach), min(6, reach), combine, 0)
    dw_ref[...] = dot_tn(flat(gs), flat(hid)).T.astype(BF16)
    lax.fori_loop(min(6, reach), reach, combine, 0)
    final = contribution(z)
    for way, chain in chains:
        cb_landed(way, chain, reach)
        final += rbuf[way, chain, reach].astype(F32)
    ig_ref[...] = final.astype(BF16)

    def og_sent(k, carry):
        for way in (0, 1):

            @pl.when((k >= 1) & (k < reach))
            def _():
                ring_send(*og_x, way, k, k + 1).wait_send()

            @pl.when((k >= 1) & (reach + k < limit[way]))
            def _():
                ring_send(*og_x, way, reach + k, reach + k + 1).wait_send()

            @pl.when(k >= 1)
            def _():
                sib_copy(*og_sib, way, k, c).wait_send()

            @pl.when((k >= 1) & (reach + k <= limit[way]))
            def _():
                sib_copy(*og_sib, way, reach + k, c).wait_send()

        return carry

    def tok_sent(d, carry):
        for way in (0, 1):

            @pl.when(d < limit[way])
            def _():
                ring_send(*tk_x, way, d, d + 1).wait_send()

            @pl.when((d <= limit[way]) & ((d > 0) | (way == 0)))
            def _():
                sib_copy(*tk_sib, way, d, c).wait_send()

        return carry

    for way in (0, 1):
        ring_send(*og_x, way, 0, 1).wait_send()
        ring_send(*og_x, way, 0, far).wait_send()
    sib_copy(*og_sib, 0, 0, c).wait_send()
    lax.fori_loop(1, reach + 1, og_sent, 0)
    lax.fori_loop(0, half_ring + 1, tok_sent, 0)
    for k in range(1, side):
        for h in range(2):
            gu_first(h, k).wait_send()
            for j in range(side):
                gu_second(h, j, k).wait_send()

    def seq_sent(k, carry):
        for g in range(2):
            rs_copy(g, k).wait_send()
            ag_copy(g, k).wait_send()
        return carry

    lax.fori_loop(1, ns, seq_sent, 0)

    def sb_sent(i, carry):
        sb_copy(i).wait_send()
        return carry

    lax.fori_loop(0, n_chunks, sb_sent, 0)

    def cb_sent(k, carry):
        for way, chain in chains:
            if (way, chain) == (1, 1):

                @pl.when(k > 0)
                def _():
                    cb_copy(way, chain, k).wait_send()
            else:
                cb_copy(way, chain, k).wait_send()
        return carry

    lax.fori_loop(0, reach, cb_sent, 0)


def per_device(
    tokens, out_grad, expert_ids, router_probs, keep_mask, gate_saved, up_saved, w_gate, w_up, w_down
):
    nz = lax.axis_size("expert") // 2
    ns = lax.axis_size("seq")
    side = {4: 2, 16: 4}[ns]
    tok_rows, width = tokens.shape
    rows, ff = gate_saved.shape[1:]
    cap = rows // 4
    n_chunks = nz // 2
    hw = ff // 2
    reach = nz // 4
    dma = pltpu.SemaphoreType.DMA
    vmem = pl.BlockSpec(memory_space=pltpu.VMEM)
    ring = (2, nz // 2 + 1)
    out = pl.pallas_call(
        functools.partial(layer_kernel, nz, side, cap),
        out_shape=(
            jax.ShapeDtypeStruct((tok_rows, width), BF16),
            jax.ShapeDtypeStruct((width, ff), BF16),
            jax.ShapeDtypeStruct((width, ff), BF16),
            jax.ShapeDtypeStruct((ff, width), BF16),
        ),
        in_specs=[vmem] * 10,
        out_specs=(vmem,) * 4,
        scratch_shapes=[
            pltpu.VMEM((2 * nz, tok_rows + 16, width), BF16),
            pltpu.VMEM((2 * nz, tok_rows, width), BF16),
            pltpu.VMEM((ns, 2, 2, rows, hw), BF16),
            pltpu.VMEM((2 * ns, rows, hw), BF16),
            pltpu.VMEM((2, ns, rows, hw), BF16),
            pltpu.VMEM((2 * ns, rows, hw), BF16),
            pltpu.VMEM((n_chunks, rows, ff), BF16),
            pltpu.VMEM((n_chunks, rows, ff), BF16),
            pltpu.VMEM((n_chunks, rows, ff), BF16),
            pltpu.VMEM((n_chunks, rows, width), BF16),
            pltpu.VMEM((n_chunks, rows, width), BF16),
            pltpu.VMEM((n_chunks, rows, width), BF16),
            pltpu.VMEM((n_chunks, rows, width), BF16),
            pltpu.VMEM((n_chunks, 8, tok_rows), F32),
            pltpu.VMEM((nz, tok_rows, width), BF16),
            pltpu.VMEM((2, 2, reach + 1, tok_rows, width), BF16),
            dma(ring), dma(ring), dma(ring), dma(ring),
            dma(ring), dma(ring), dma(ring), dma(ring),
            dma((2, side + 1, side)), dma((2, side + 1, side)),
            dma((2, ns)), dma((2, ns)), dma((2, ns)), dma((2, ns)),
            dma((n_chunks,)), dma((n_chunks,)),
            dma((2, 2, reach + 1)), dma((2, 2, reach + 1)),
        ],
        compiler_params=pltpu.CompilerParams(
            collective_id=0, has_side_effects=True, vmem_limit_bytes=56 << 20
        ),
        cost_estimate=pl.CostEstimate(flops=3 << 30, bytes_accessed=4 << 20, transcendentals=1 << 20),
    )(
        tokens, out_grad, expert_ids.T, router_probs.T, keep_mask.T, gate_saved[0], up_saved[0],
        w_gate[0], w_up[0], w_down[0],
    )
    return (out[0], out[1][None], out[2][None], out[3][None])


def solution(mesh):
    return jax.shard_map(
        per_device,
        mesh=mesh,
        in_specs=(
            P("expert", "seq"),
            P("expert", "seq"),
            P("expert", None),
            P("expert", None),
            P("expert", None),
            P("expert", "seq", None),
            P("expert", "seq", None),
            P("expert", "seq", None),
            P("expert", "seq", None),
            P("expert", None, "seq"),
        ),
        out_specs=(
            P("expert", "seq"),
            P("expert", "seq", None),
            P("expert", "seq", None),
            P("expert", None, "seq"),
        ),
        check_vma=False,
    )
```

time: 546 us -> 197 us (0.36)
  the two profiles are of different devices: /device:TPU:1 before, /device:TPU:64 now
where the time goes in v1:
time: 197 us; the launch traced here: 196 us
  Pallas kernels  191 us (97%)
  local copies, waits for them, and re-layouts  5.18 us (3%)
    pallas_call x1, Pallas kernels, per_device(): pl.pallas_call(functools.partial(layer_kernel, nz, side, cap), out_shape=...  191 us
    unnamed x8, local copies, waits for them, and re-layouts  5.18 us

profile of v1, /device:TPU:64, one launch (start us, length us, event | category | flops | bytes accessed | tf_op | source)
XLA Modules:
  0.0 196.5 jit_solution(16843559456771868934)
XLA Ops:
  0.6 190.6 %shard_map.129 = (bf16[128,256]{1,0:T(8,128)(2,1)}, bf16[256,768]{1,0:T(8,128)(2,1)}, bf16[256,768]{1,0:T(8,128)(2,1)}, bf16[768,256]{1,0:T(8,128)(2,1)}) custom-call(bf16[128,256]{1,0:T(8,128)(2,1)} %tok_ref.1, bf16[128,256]{1,0:T(8,128)(2,1)} %og_ref.1, s32[8,128]{1,0:T(8,128)} %bitcast.19, f32[8,128]{1,0:T(8,128)} %bitcast.20, s32[8,128]{1,0:T(8,128)} %bitcast.21, ...), custom_call_target="tpu_custom_call" | custom-call | flops 3221225472 | bytes 4194304 | tf_op jit(solution)/shard_map/pallas_call | solution.py:583
  191.3 1.5 copy.18
  192.8 0.0 copy-start.1
  192.8 1.8 copy.19
  194.6 0.0 copy-done.1
  194.6 0.0 copy-start
  194.6 0.7 copy.20
  195.3 0.4 copy-done
  195.7 0.7 copy.21
Async XLA Ops:
  192.8 1.8 copy-start.1
  194.6 1.1 copy-start

commit v2 on v1

--- a/solution.py
+++ b/solution.py
@@ -26,11 +26,11 @@
 
 def layer_kernel(
     nz, side, cap,
-    tok_ref, og_ref, ids_ref, prob_ref, keep_ref, gate_ref, up_ref, wg_ref, wu_ref, wd_ref,
+    tok_ref, og_ref, ids_in, prob_in, keep_in, gate_ref, up_ref, wg_in, wu_in, wd_in,
     ig_ref, gw_ref, uw_ref, dw_ref,
     og_all, tok_all, gu_all, pbuf, rsbuf, hg_all, gg, ug, hid, gs, xs, sb, sbs, pos_ref, contrib, rbuf,
     og_s, og_r, og_ss, og_sr, tk_s, tk_r, tk_ss, tk_sr, gu_s, gu_r, rs_s, rs_r, ag_s, ag_r, sb_s, sb_r,
-    cb_s, cb_r,
+    cb_s, cb_r, ids_ref, prob_ref, keep_ref, wg_ref, wu_ref, wd_ref, load_s,
 ):
     ns = side * side
     ec = lax.axis_index("expert")
@@ -59,6 +59,21 @@
             src, dst, ssem, rsem, device_id=device, device_id_type=MESH
         )
 
+    small = [(ids_in, ids_ref), (prob_in, prob_ref), (keep_in, keep_ref)]
+    small += [(og_ref, og_all.at[ec, pl.ds(0, tok_rows)]), (tok_ref, tok_all.at[ec])]
+    saved = [
+        (ref.at[:, pl.ds(h * hw, hw)], gu_all.at[s, h, a])
+        for h in range(2)
+        for a, ref in ((0, gate_ref), (1, up_ref))
+    ]
+    large = [(wd_in, wd_ref), (wg_in, wg_ref), (wu_in, wu_ref)]
+    loads = [
+        pltpu.make_async_copy(src, dst, load_s.at[n])
+        for n, (src, dst) in enumerate(small + saved + large)
+    ]
+    for load in loads:
+        load.start()
+
     bar = pltpu.get_barrier_semaphore()
     hops = sorted({1, nz - 1, far, nz - far})
     for k in hops:
@@ -71,18 +86,15 @@
 
     lax.fori_loop(1, ns, greet, 0)
 
+    for load in loads[:5]:
+        load.wait()
     weight = prob_ref[...] * keep_ref[...].astype(F32)
     w_hi = weight.astype(BF16).astype(F32)
     w_mid = (weight - w_hi).astype(BF16).astype(F32)
     w_lo = (weight - w_hi) - w_mid
     top = jnp.concatenate([ids_ref[...].astype(F32), w_mid], axis=1)
     low = jnp.concatenate([w_hi, w_lo], axis=1)
-    og_all[ec, pl.ds(0, tok_rows), :] = og_ref[...]
     og_all[ec, pl.ds(tok_rows, 16), :] = jnp.concatenate([top, low], axis=0).astype(BF16)
-    tok_all[ec] = tok_ref[...]
-    for h in range(2):
-        gu_all[s, h, 0] = gate_ref[:, h * hw : (h + 1) * hw]
-        gu_all[s, h, 1] = up_ref[:, h * hw : (h + 1) * hw]
     pl.semaphore_wait(bar, len(hops) + 1 + ns - 1)
 
     def zslot(way, d, core):
@@ -139,6 +151,8 @@
         ref = gu_all.at[slot, h]
         remote(ref, ref, gu_s.at[h, a, k], gu_r.at[h, a, k], dev(ec, s)).wait_recv()
 
+    for load in loads[5:9]:
+        load.wait()
     for k in range(1, side):
         for h in range(2):
             gu_first(h, k).start()
@@ -361,6 +375,7 @@
         partial_products(4 * m - 4, 4)
         return carry
 
+    loads[9].wait()
     lax.fori_loop(1, quarter - 1, two_steps, 0)
     rs_start(0)
     two_steps(quarter - 1, 0)
@@ -380,6 +395,8 @@
                 m = side - k
                 slot = seq_of(sy + m, sx + j) if h == 0 else seq_of(sy + j, sx + m)
                 gu_landed(slot, h, 1 + j, k)
+    loads[10].wait()
+    loads[11].wait()
     activations(0)
     activations(1)
     lax.fori_loop(reach + 5, half_ring + 1, tok_step, 0)
@@ -588,7 +605,7 @@
             jax.ShapeDtypeStruct((width, ff), BF16),
             jax.ShapeDtypeStruct((ff, width), BF16),
         ),
-        in_specs=[vmem] * 10,
+        in_specs=[pl.BlockSpec(memory_space=pltpu.HBM)] * 10,
         out_specs=(vmem,) * 4,
         scratch_shapes=[
             pltpu.VMEM((2 * nz, tok_rows + 16, width), BF16),
@@ -613,6 +630,12 @@
             dma((2, ns)), dma((2, ns)), dma((2, ns)), dma((2, ns)),
             dma((n_chunks,)), dma((n_chunks,)),
             dma((2, 2, reach + 1)), dma((2, 2, reach + 1)),
+            pltpu.VMEM(expert_ids.shape[::-1], jnp.int32),
+            pltpu.VMEM(router_probs.shape[::-1], F32),
+            pltpu.VMEM(keep_mask.shape[::-1], jnp.int32),
+            pltpu.VMEM((width, ff), BF16), pltpu.VMEM((width, ff), BF16),
+            pltpu.VMEM((ff, width), BF16),
+            dma((12,)),
         ],
         compiler_params=pltpu.CompilerParams(
             collective_id=0, has_side_effects=True, vmem_limit_bytes=56 << 20

time: 197 us -> 195 us (0.990)
  Pallas kernels: 191 us -> 189 us
    pallas_call x1, Pallas kernels: 191 us -> 189 us  [per_device(): pl.pallas_call(functools.partial(layer_kernel, nz, side, cap), out_shape=...]
where the time goes in v2:
time: 195 us; the launch traced here: 194 us
  Pallas kernels  189 us (97%)
  local copies, waits for them, and re-layouts  5.18 us (3%)
    pallas_call x1, Pallas kernels, per_device(): pl.pallas_call(functools.partial(layer_kernel, nz, side, cap), out_shape=...  189 us
    unnamed x8, local copies, waits for them, and re-layouts  5.18 us

profile of v2, /device:TPU:64, one launch (start us, length us, event | category | flops | bytes accessed | tf_op | source)
XLA Modules:
  0.0 194.4 jit_solution(5685042558109432469)
XLA Ops:
  0.6 188.6 %shard_map.129 = (bf16[128,256]{1,0:T(8,128)(2,1)}, bf16[256,768]{1,0:T(8,128)(2,1)}, bf16[256,768]{1,0:T(8,128)(2,1)}, bf16[768,256]{1,0:T(8,128)(2,1)}) custom-call(bf16[128,256]{1,0:T(8,128)(2,1)} %tok_ref.1, bf16[128,256]{1,0:T(8,128)(2,1)} %og_ref.1, s32[8,128]{1,0:T(8,128)} %bitcast.19, f32[8,128]{1,0:T(8,128)} %bitcast.20, s32[8,128]{1,0:T(8,128)} %bitcast.21, ...), custom_call_target="tpu_custom_call" | custom-call | flops 3221225472 | bytes 4194304 | tf_op jit(solution)/shard_map/pallas_call | solution.py:600
  189.2 1.5 copy.18
  190.7 0.0 copy-start.1
  190.7 1.8 copy.19
  192.5 0.0 copy-done.1
  192.5 0.0 copy-start
  192.5 0.7 copy.20
  193.2 0.4 copy-done
  193.6 0.7 copy.21
Async XLA Ops:
  190.7 1.8 copy-start.1
  192.5 1.1 copy-start
